TPU v7x, 256 devices: a whole 4x4x8 slice. The times are simulated.
256 devices in a mesh: rows: 32 (over y, z), own: 8 (over x, core).
Axes of the slice: x: 4, y: 4, z: 8, core: 2. Of those that a mesh axis runs over, the one named last changes fastest.
Arguments:
- embedding: bfloat16 [1048576, 128], P(('rows', 'own')), may hold values from -6 to 6
- assignment: int32 [1048576, 1], P(('rows', 'own')), may hold values from 0 to 1023; in each aligned block of 4096 rows (0 to 4095, 4096 to 8191, ...) at most 8 rows name the same one
- sub_logit: float32 [512], P('own'), may hold values from -1 to 1
- merge_offset: int32 [512], P(('own', 'rows')), may hold values from 1 to 7
Outputs:
- sub_prob: float32 [1048576], P(('rows', 'own'))
- split_score: float32 [512], P(('own', 'rows'))
- merge_score: float32 [512], P(('own', 'rows'))
Inputs may be any that keep to these rules, and one draw needn't show every extreme that they name: `assignment`: within the 4096 rows of one device (aligned blocks) no id is named by more than 8 rows, a bound that some block reaches; every id is named somewhere.
All inputs are finite; a program needn't handle non-finite values.
Results may differ from a plain program's by a relative error of at most 0.0003.
Values may be sent and summed in bfloat16 or wider, within the bound.
No kernel may reach another device: no remote copies, remote signals or barrier semaphores. Data moves between devices by JAX's collectives and lax.ppermute only.
A program may use at most 64 MiB of HBM per device.

v0:
```python
import math

import jax
import jax.numpy as jnp
from jax import lax
from jax.experimental import pallas as pl
from jax.experimental.pallas import tpu as pltpu
from jax.sharding import PartitionSpec as P

D = 128
CAP = 8
EMPTY = 64.0
VMEM_LIMIT = 48 * 1024 * 1024
WIDE_LIMIT = 60 * 1024 * 1024
MERGE_FLOPS = 1
FAR = 8
NARROW_LIMIT = 16 * 1024 * 1024
PANEL = 16
STEP = 4
PIECES = 4


def iota(shape, dim):
    return lax.broadcasted_iota(jnp.int32, shape, dim)


def split3(value):
    high = value.astype(jnp.bfloat16)
    rest = value - high.astype(jnp.float32)
    middle = rest.astype(jnp.bfloat16)
    low = (rest - middle.astype(jnp.float32)).astype(jnp.bfloat16)
    return high, middle, low


def slots_of(labels):
    blocks = labels.shape[0]
    flipped = jnp.transpose(labels.astype(jnp.float32))
    before = iota((128, 128), 0) < iota((128, 128), 1)
    lanes = iota((128, 128), 1)
    levels = iota((8, 128), 0)
    running = jnp.zeros((8, 128), jnp.float32)
    rows = []
    for b in range(blocks):
        across = labels[b : b + 1, :]
        down = jnp.broadcast_to(flipped[:, b : b + 1], (128, 128)).astype(jnp.int32)
        same = jnp.where((down == across) & before, 1.0, 0.0)
        inside = jnp.sum(same, axis=0, keepdims=True)
        low = across & 127
        upper = levels == (across >> 7)
        found = jnp.take_along_axis(running, jnp.broadcast_to(low, (8, 128)), axis=1)
        earlier = jnp.sum(jnp.where(upper, found, 0.0), axis=0, keepdims=True)
        rows.append(across * CAP + (inside + earlier).astype(jnp.int32))
        hot_low = jnp.where((down & 127) == lanes, 1.0, 0.0).astype(jnp.bfloat16)
        hot_up = jnp.where(upper, 1.0, 0.0).astype(jnp.bfloat16)
        running = running + jnp.dot(hot_up, hot_low, preferred_element_type=jnp.float32)
    return jnp.concatenate(rows, axis=0)


def dispatch_kernel(labels_ref, rows_ref, target_ref, out_ref, held, rows, wide, table, ready, places, sems):
    load_labels = pltpu.make_async_copy(labels_ref, held, sems.at[0])
    load_labels.start()
    load_rows = pltpu.make_async_copy(rows_ref, rows, sems.at[1])
    load_rows.start()
    table[...] = jnp.full(table.shape, EMPTY, jnp.float32)
    load_labels.wait()
    target_ref[...] = slots_of(held[...])
    copy = pltpu.make_async_copy(target_ref, places, sems.at[2])
    copy.start()
    load_rows.wait()
    wide[...] = rows[...].astype(jnp.float32)
    copy.wait()

    def block(b, carry):
        for j in range(128):
            table[pl.ds(places[b, j], 1), :] = wide[pl.ds(b * 128 + j, 1), :]
        return carry

    lax.fori_loop(0, held.shape[0], block, 0)
    piece = table.shape[0] // PIECES
    stores = []
    for k in range(PIECES):
        part = pl.ds(k * piece, piece)
        ready[part, :] = table[part, :].astype(jnp.bfloat16)
        stores.append(pltpu.make_async_copy(ready.at[part], out_ref.at[part], sems.at[3 + k]))
        stores[-1].start()
    for store in stores:
        store.wait()


def dispatch(embedding, labels, slots):
    total = embedding.shape[0]
    return pl.pallas_call(
        dispatch_kernel,
        out_shape=(
            jax.ShapeDtypeStruct(labels.shape, jnp.int32),
            jax.ShapeDtypeStruct((slots, D), jnp.bfloat16),
        ),
        in_specs=[pl.BlockSpec(memory_space=pltpu.HBM)] * 2,
        out_specs=[
            pl.BlockSpec(memory_space=pltpu.VMEM),
            pl.BlockSpec(memory_space=pltpu.HBM),
        ],
        scratch_shapes=[
            pltpu.VMEM(labels.shape, jnp.int32),
            pltpu.VMEM((total, D), jnp.bfloat16),
            pltpu.VMEM((total, D), jnp.float32),
            pltpu.VMEM((slots, D), jnp.float32),
            pltpu.VMEM((slots, D), jnp.bfloat16),
            pltpu.SMEM(labels.shape, jnp.int32),
            pltpu.SemaphoreType.DMA((3 + PIECES,)),
        ],
        compiler_params=pltpu.CompilerParams(vmem_limit_bytes=WIDE_LIMIT),
    )(labels, embedding)


def eliminate(work, count):
    pivots = [[] for _ in range(count)]
    lanes = iota((PANEL, D), 1)
    down = iota((PANEL, D), 0)
    for p in range(D // PANEL):
        base = p * PANEL
        tiles = [work[m, base : base + PANEL, :] for m in range(count)]
        diag = [jnp.ones((PANEL, D), jnp.float32) for _ in range(count)]
        for i in range(0, PANEL, STEP):
            inside = (lanes >= base + i) & (lanes < base + i + STEP)
            unit = jnp.where(lanes - base == down, 1.0, 0.0)
            for m in range(count):
                tile = tiles[m]
                columns = [
                    jnp.broadcast_to(tile[:, base + i + t : base + i + t + 1], (PANEL, D))
                    for t in range(STEP)
                ]
                small = [
                    [columns[v][i + t : i + t + 1, :] for v in range(STEP)] for t in range(STEP)
                ]
                tile = jnp.where(inside, unit, tile)
                lines = [tile[i + t : i + t + 1, :] for t in range(STEP)]
                for t in range(STEP):
                    inverse = 1.0 / small[t][t]
                    diag[m] = jnp.where(down == i + t, small[t][t], diag[m])
                    for u in range(t + 1, STEP):
                        ratio = small[t][u] * inverse
                        for v in range(u, STEP):
                            small[u][v] = small[u][v] - ratio * small[t][v]
                        columns[u] = columns[u] - ratio * columns[t]
                        lines[u] = lines[u] - ratio * lines[t]
                    factor = jnp.where(down > i + t, columns[t] * inverse, 0.0)
                    tile = tile - factor * lines[t]
                tiles[m] = tile
        for m in range(count):
            pivots[m].append(diag[m])
            work[m, base : base + PANEL, :] = tiles[m]
            below = base + PANEL
            if below < D:
                e1, e2, e3 = split3(tiles[m])
                n1, n2, n3 = split3(tiles[m] * (1.0 / diag[m]))
                left = jnp.concatenate([n1, n1, n2, n2, n1, n3], axis=0)
                right = jnp.concatenate([e1, e2, e1, e2, e3, e1], axis=0)
                step = lax.dot_general(
                    left,
                    right,
                    (((0,), (0,)), ((), ())),
                    preferred_element_type=jnp.float32,
                )
                old = work[m, below:, :]
                wide_lanes = iota(old.shape, 1)
                within = (wide_lanes >= base) & (wide_lanes < below)
                work[m, below:, :] = jnp.where(within, 0.0, old) - step[below:, :]
    return pivots


def log_sum(pivot_tiles):
    total = jnp.zeros((1, D), jnp.float32)
    for tile in pivot_tiles:
        total = total + jnp.sum(jnp.log(tile), axis=0, keepdims=True)
    return total


def posterior_scatter(second, first, number):
    same = iota((D, D), 0) == iota((D, D), 1)
    over = jnp.broadcast_to(first, (D, D))
    return jnp.where(same, 1.0, 0.0) + second - jnp.transpose(over) * over / (1.0 + number)


def moments_kernel(rows_ref, xt_ref, second_ref, info_ref, pack_ref, turned_ref, sems):
    stores = []
    depth = rows_ref.shape[0] * 16
    moments = []
    for c in range(2):
        rows = rows_ref[:, 16 * c : 16 * c + 16, :].reshape(depth, D)
        empty = rows.astype(jnp.float32) > 8.0
        clean = jnp.where(empty, 0.0, rows.astype(jnp.float32)).astype(jnp.bfloat16)
        valid = jnp.where(empty, 0.0, 1.0).astype(jnp.bfloat16)
        turned = jnp.transpose(clean)
        turned_ref[c] = turned
        stores.append(pltpu.make_async_copy(turned_ref.at[c], xt_ref.at[c], sems.at[c]))
        stores[c].start()
        zero_side = (iota((D, depth), 1) & 8) == 0
        none = jnp.zeros_like(turned)
        left = jnp.concatenate(
            [jnp.where(zero_side, turned, none), jnp.where(zero_side, none, turned)], axis=0
        )
        second = jnp.dot(left, clean, preferred_element_type=jnp.float32)
        side = ((iota((16, depth), 1) >> 3) & 1) == (iota((16, depth), 0) & 1)
        pick = jnp.where(side, 1.0, 0.0).astype(jnp.bfloat16)
        first = jnp.dot(pick, clean, preferred_element_type=jnp.float32)
        number = jnp.dot(pick, valid, preferred_element_type=jnp.float32)
        for s in range(2):
            m = 2 * c + s
            moments.append((second[s * D : (s + 1) * D], first[s : s + 1], number[s : s + 1]))
            second_ref[m] = moments[m][0]
    info_ref[...] = jnp.concatenate(
        [moments[m][1] for m in range(4)] + [moments[m][2] for m in range(4)], axis=0
    )
    whole = [tuple(a + b for a, b in zip(moments[2 * c], moments[2 * c + 1])) for c in range(2)]
    lower = iota((D, D), 0) >= iota((D, D), 1)
    same = iota((D, D), 0) == iota((D, D), 1)
    packed = jnp.where(lower, whole[0][0], whole[1][0])
    diagonal = jnp.sum(jnp.where(same, whole[1][0], 0.0), axis=0, keepdims=True)
    ending = jnp.concatenate(
        [diagonal, whole[0][1], whole[1][1], whole[0][2], whole[1][2], jnp.zeros((3, D), jnp.float32)],
        axis=0,
    )
    for q in range(pack_ref.shape[0]):
        pack_ref[q, 0:D, :] = packed
        pack_ref[q, D : D + 8, :] = ending
    for store in stores:
        store.wait()


def find_moments(arrived, owners):
    depth = arrived.shape[0] * 16
    f32 = jnp.float32
    return pl.pallas_call(
        moments_kernel,
        out_shape=(
            jax.ShapeDtypeStruct((FAR, D, depth), jnp.bfloat16),
            jax.ShapeDtypeStruct((4, D, D), f32),
            jax.ShapeDtypeStruct((8, D), f32),
            jax.ShapeDtypeStruct((owners, D + 8, D), f32),
        ),
        in_specs=[pl.BlockSpec(memory_space=pltpu.VMEM)],
        out_specs=[pl.BlockSpec(memory_space=pltpu.HBM)]
        + [pl.BlockSpec(memory_space=pltpu.VMEM)] * 3,
        scratch_shapes=[
            pltpu.VMEM((2, D, depth), jnp.bfloat16),
            pltpu.SemaphoreType.DMA((2,)),
        ],
        compiler_params=pltpu.CompilerParams(vmem_limit_bytes=VMEM_LIMIT),
        cost_estimate=pl.CostEstimate(flops=10**9, bytes_accessed=4 * 10**6, transcendentals=0),
    )(arrived)


def judge_kernel(logit_ref, far_ref, second_ref, info_ref, odds_ref, dets_ref, work, lines, xt_ref, sem):
    load = pltpu.make_async_copy(far_ref.at[0:2], xt_ref, sem)
    load.start()
    clusters, _, depth = xt_ref.shape
    firsts = [info_ref[m : m + 1, :] for m in range(4)]
    numbers = [info_ref[m : m + 1, :] for m in range(4, 8)]
    for m in range(4):
        work[m] = posterior_scatter(second_ref[m], firsts[m], numbers[m])
    pivots = eliminate(work, 4)
    logdets = [log_sum(tiles) for tiles in pivots]
    dets_ref[...] = jnp.concatenate(logdets + numbers, axis=0)
    lower = iota((D, D), 0) >= iota((D, D), 1)
    lanes = iota((depth // 128, 128), 1)
    width = min(512, depth)
    odds = []
    load.wait()
    for c in range(clusters):
        offsets, shifts, pieces = [], [], []
        for t in range(2):
            m = 2 * c + t
            spread = jnp.concatenate(pivots[m], axis=0)
            unit = jnp.where(lower, work[m], 0.0)
            whiten = jnp.sqrt(numbers[m] + 2.0) * (unit * lax.rsqrt(spread))
            center = firsts[m] / (1.0 + numbers[m])
            shifted = jnp.sum(whiten * center, axis=1, keepdims=True)
            shifts.append(jnp.broadcast_to(shifted, (D, width)))
            pieces.append(jnp.concatenate(split3(whiten), axis=1))
            offsets.append(0.5 * D * jnp.log(numbers[m] + 2.0) - 0.5 * logdets[m])
        maps = jnp.concatenate(pieces, axis=0)
        shift = jnp.concatenate(shifts, axis=0)
        base = logit_ref[c] + (offsets[1] - offsets[0])
        for w in range(depth // width):
            columns = xt_ref[c, :, w * width : (w + 1) * width]
            image = jnp.dot(
                maps, jnp.concatenate([columns] * 3, axis=0), preferred_element_type=jnp.float32
            )
            image = image - shift
            squares = image * image
            gap = jnp.sum(squares[:D] - squares[D:], axis=0, keepdims=True)
            for v in range(width // 128):
                row = w * (width // 128) + v
                lines[row : row + 1, :] = gap[:, v * 128 : (v + 1) * 128]
        odds.append(1.0 / (1.0 + jnp.exp(-(base + 0.5 * lines[...]))))
    for s in range(8):
        first = pltpu.roll(odds[0], (128 - 16 * s) % 128, 1)
        second = pltpu.roll(odds[1], (144 - 16 * s) % 128, 1)
        odds_ref[pl.ds(s, depth // 128, stride=8), :] = jnp.where(lanes < 16, first, second)


def judge(logits, xt, second, info):
    depth = xt.shape[2]
    f32 = jnp.float32
    return pl.pallas_call(
        judge_kernel,
        out_shape=(
            jax.ShapeDtypeStruct((depth // 16, 128), f32),
            jax.ShapeDtypeStruct((8, D), f32),
        ),
        in_specs=[
            pl.BlockSpec(memory_space=pltpu.SMEM),
            pl.BlockSpec(memory_space=pltpu.HBM),
            pl.BlockSpec(memory_space=pltpu.VMEM),
            pl.BlockSpec(memory_space=pltpu.VMEM),
        ],
        out_specs=[pl.BlockSpec(memory_space=pltpu.VMEM)] * 2,
        scratch_shapes=[
            pltpu.VMEM((4, D, D), f32),
            pltpu.VMEM((depth // 128, 128), f32),
            pltpu.VMEM((2, D, depth), jnp.bfloat16),
            pltpu.SemaphoreType.DMA,
        ],
        compiler_params=pltpu.CompilerParams(vmem_limit_bytes=VMEM_LIMIT),
        cost_estimate=pl.CostEstimate(flops=10**10, bytes_accessed=10**7, transcendentals=0),
    )(logits, xt, second, info)


def unpack(pack):
    body = pack[0:D]
    flipped = jnp.transpose(body)
    low = iota((D, D), 0) > iota((D, D), 1)
    same = iota((D, D), 0) == iota((D, D), 1)
    second0 = jnp.where(low, body, flipped)
    second1 = jnp.where(same, pack[D : D + 1], jnp.where(low, flipped, body))
    return (
        (second0, pack[D + 1 : D + 2], pack[D + 3 : D + 4]),
        (second1, pack[D + 2 : D + 3], pack[D + 4 : D + 5]),
    )


def log_gamma(x):
    z = x + 8.0
    inverse = 1.0 / z
    square = inverse * inverse
    series = inverse * (1.0 / 12.0 - square * (1.0 / 360.0 - square * (1.0 / 1260.0)))
    low = x * (x + 1.0) * (x + 2.0) * (x + 3.0)
    high = (x + 4.0) * (x + 5.0) * (x + 6.0) * (x + 7.0)
    half_log_tau = 0.5 * math.log(2.0 * math.pi)
    return (z - 0.5) * jnp.log(z) - z + half_log_tau + series - jnp.log(low) - jnp.log(high)


def evidence(numbers, logdets):
    prior = D + 3.0
    half_steps = 0.5 * iota(numbers.shape, 1).astype(jnp.float32)
    terms = log_gamma(0.5 * (prior + numbers) - half_steps) - log_gamma(0.5 * prior - half_steps)
    return (
        -0.5 * D * math.log(math.pi) * numbers
        + jnp.sum(terms, axis=1, keepdims=True)
        - 0.5 * (prior + numbers) * logdets
        - 0.5 * D * jnp.log(1.0 + numbers)
        + log_gamma(numbers)
    )


def merge_kernel(mate_ref, dets_ref, own_ref, mate0_ref, mate1_ref, split_ref, join_ref, work):
    own = unpack(own_ref[...])
    mates = (unpack(mate0_ref[...])[0], unpack(mate1_ref[...])[1])
    both = tuple(tuple(a + b for a, b in zip(own[c], mates[c])) for c in range(2))
    stats = own + mates + both
    for m in range(6):
        work[m] = posterior_scatter(*stats[m])
    pivots = eliminate(work, 6)
    blank = [jnp.ones((6, D), jnp.float32)]
    numbers = jnp.concatenate([dets_ref[4:8, :]] + [stats[m][2] for m in range(6)] + blank, axis=0)
    logdets = jnp.concatenate([dets_ref[0:4, :]] + [log_sum(pivots[m]) for m in range(6)] + blank, axis=0)
    value = evidence(numbers, logdets)
    for c in range(2):
        whole = value[4 + c : 5 + c]
        split = value[2 * c : 2 * c + 1] + value[2 * c + 1 : 2 * c + 2] - whole
        join = value[8 + c : 9 + c] - whole - value[6 + c : 7 + c]
        split_ref[c] = split[0, 0] * (1.0 / (D * D))
        join_ref[c] = join[0, 0] * (1.0 / (D * D))


def merge(mate, dets, own, everyone):
    block = (None,) + own.shape[1:]
    one = jax.ShapeDtypeStruct((2,), jnp.float32)
    return pl.pallas_call(
        merge_kernel,
        out_shape=(one, one),
        grid_spec=pltpu.PrefetchScalarGridSpec(
            num_scalar_prefetch=1,
            grid=(1,),
            in_specs=[
                pl.BlockSpec(dets.shape, lambda g, mate: (0, 0)),
                pl.BlockSpec(block, lambda g, mate: (0, 0, 0)),
                pl.BlockSpec(block, lambda g, mate: (mate[0], 0, 0)),
                pl.BlockSpec(block, lambda g, mate: (mate[1], 0, 0)),
            ],
            out_specs=[pl.BlockSpec(memory_space=pltpu.SMEM)] * 2,
            scratch_shapes=[pltpu.VMEM((6, D, D), jnp.float32)],
        ),
        compiler_params=pltpu.CompilerParams(vmem_limit_bytes=NARROW_LIMIT),
        cost_estimate=pl.CostEstimate(flops=MERGE_FLOPS, bytes_accessed=1, transcendentals=0),
    )(mate, dets, own, everyone, everyone)


def read_kernel(table_ref, target_ref, out_ref, lines):
    depth = table_ref.shape[0] // 4
    lanes = iota((depth, 128), 1)
    total = table_ref[pl.ds(0, depth, stride=4), 0, :]
    for q in range(1, 4):
        moved = pltpu.roll(table_ref[pl.ds(q, depth, stride=4), 0, :], 32 * q, 1)
        total = jnp.where(lanes >= 32 * q, moved, total)
    lines[...] = total
    target = target_ref[...]
    upper = target >> 7
    low = target & 127
    for g in range(target.shape[0] // 8):
        part = slice(8 * g, 8 * g + 8)
        total = jnp.zeros((8, 128), jnp.float32)
        for k in range(depth):
            line = jnp.broadcast_to(lines[k : k + 1, :], (8, 128))
            found = jnp.take_along_axis(line, low[part], axis=1)
            total = jnp.where(upper[part] == k, found, total)
        out_ref[part, :] = total


def read_back(table, target):
    return pl.pallas_call(
        read_kernel,
        out_shape=jax.ShapeDtypeStruct(target.shape, jnp.float32),
        scratch_shapes=[pltpu.VMEM((table.shape[0] // 4, 128), jnp.float32)],
        compiler_params=pltpu.CompilerParams(vmem_limit_bytes=NARROW_LIMIT),
    )(table, target)


def shards(embedding, assignment, sub_logit, merge_offset):
    owners, holders = lax.axis_size("own"), lax.axis_size("rows")
    experts = 2 * owners * sub_logit.shape[0]
    axes = ("own", "rows")
    devices = owners * holders
    labels = assignment.reshape(-1, 128)
    target, outgoing = dispatch(embedding, labels, experts * CAP)
    per_holder = merge_offset.shape[0]
    chunk = 2 * per_holder * CAP
    arrived = lax.all_to_all(
        outgoing.reshape(devices, chunk, D), axes, split_axis=0, concat_axis=0, tiled=True
    )
    logits = lax.dynamic_slice(sub_logit, (lax.axis_index("rows") * per_holder,), (per_holder,))
    xt, second, info, packs = find_moments(arrived, owners)
    everyone = lax.all_to_all(packs, "own", split_axis=0, concat_axis=0, tiled=True)
    odds, dets = judge(logits, xt, second, info)
    odds, everyone = lax.optimization_barrier((odds, everyone))
    returned = lax.all_to_all(
        odds.reshape(devices, 1, 128), axes, split_axis=0, concat_axis=0, tiled=True
    )
    mate = (lax.axis_index("own") + merge_offset) % owners
    split, join = merge(mate, dets, packs, everyone)
    sub_prob = read_back(returned, target).reshape(-1)
    return (sub_prob, split, join)


def solution(mesh):
    in_specs = (P(("rows", "own"), None), P(("rows", "own"), None), P("own"), P(("own", "rows")))
    out_specs = (P(("rows", "own")), P(("own", "rows")), P(("own", "rows")))
    return jax.shard_map(shards, mesh=mesh, in_specs=in_specs, out_specs=out_specs, check_vma=False)
```

profile of v0, /device:TPU:1, one launch (start us, length us, event | category | flops | bytes accessed | tf_op | source)
XLA Modules:
  0.0 119.0 jit_solution(14768821906383550604)
XLA Ops:
  0.6 8.6 %shard_map.67 = (s32[32,128]{1,0:T(8,128)}, bf16[8192,128]{1,0:T(8,128)(2,1)}) custom-call(s32[32,128]{1,0:T(8,128)} %bitcast.5, bf16[4096,128]{1,0:T(8,128)(2,1)} %rows_ref.1), custom_call_target="tpu_custom_call" | custom-call | tf_op jit(solution)/shard_map/pallas_call | solution.py:92
  9.2 0.0 copy-start.1
  9.2 15.7 %all-to-all-start = ((bf16[256,32,128]{2,1,0:T(8,128)(2,1)}), bf16[256,32,128]{2,1,0:T(8,128)(2,1)S(1)}, u32[]{:S(2)}, u32[]{:S(2)}) async-start(bf16[256,32,128]{2,1,0:T(8,128)(2,1)} %bitcast.4), calls=%async_computation | async-start | bytes 4194304 | tf_op jit(solution)/shard_map/all_to_all | solution.py:449
  24.9 0.0 copy-done.1
  24.9 0.1 dynamic_slice.3.logit_ref
  25.0 54.2 %all-to-all-done.rows_ref = bf16[256,32,128]{2,1,0:T(8,128)(2,1)S(1)} async-done(((bf16[256,32,128]{2,1,0:T(8,128)(2,1)}), bf16[256,32,128]{2,1,0:T(8,128)(2,1)S(1)}, u32[]{:S(2)}, u32[]{:S(2)}) %all-to-all-start) | async-done | bytes 2097184 | tf_op jit(solution)/shard_map/all_to_all | solution.py:449
  79.2 3.8 %shard_map.68 = (bf16[8,128,4096]{2,1,0:T(8,128)(2,1)}, f32[4,128,128]{2,1,0:T(8,128)S(1)}, f32[8,128]{1,0:T(8,128)S(1)}, f32[8,136,128]{2,1,0:T(8,128)}) custom-call(bf16[256,32,128]{2,1,0:T(8,128)(2,1)S(1)} %all-to-all-done.rows_ref), custom_call_target="tpu_custom_call" | custom-call | flops 1000000000 | bytes 4000000 | tf_op jit(solution)/shard_map/pallas_call | solution.py:234
  83.1 3.5 %all-to-all-start.1 = ((f32[8,136,128]{2,1,0:T(8,128)}), f32[8,136,128]{2,1,0:T(8,128)S(1)}, u32[]{:S(2)}, u32[]{:S(2)}) async-start(f32[8,136,128]{2,1,0:T(8,128)} %get-tuple-element.20.own_ref), calls=%async_computation.1 | async-start | bytes 1114112 | tf_op jit(solution)/shard_map/all_to_all | solution.py:454
  86.6 0.0 copy-start.2
  86.6 0.0 copy-start
  86.6 10.3 %shard_map.69 = (f32[256,128]{1,0:T(8,128)}, f32[8,128]{1,0:T(8,128)S(1)}) custom-call(f32[2]{0:T(128)S(1)} %dynamic_slice.3.logit_ref, bf16[8,128,4096]{2,1,0:T(8,128)(2,1)} %get-tuple-element.16.far_ref, f32[4,128,128]{2,1,0:T(8,128)S(1)} %get-tuple-element.17.second_ref, f32[8,128]{1,0:T(8,128)S(1)} %get-tuple-element.18.info_ref), custom_call_target="tpu_custom_call" | custom-call | flops 10000000000 | bytes 10000000 | tf_op jit(solution)/shard_map/pallas_call | solution.py:306
  96.9 0.0 all-to-all-done.1.mate0_ref.mate1_ref
  96.9 8.0 %all-to-all-start.2 = ((f32[256,1,128]{2,1,0:T(1,128)}), f32[256,1,128]{2,1,0:T(1,128)S(1)}, u32[]{:S(2)}, u32[]{:S(2)}) async-start(f32[256,1,128]{2,1,0:T(1,128)} %bitcast.2), calls=%async_computation.2 | async-start | bytes 262144 | tf_op jit(solution)/shard_map/all_to_all | solution.py:457
  104.9 0.0 copy-done.2
  104.9 8.3 %shard_map.71 = (f32[2]{0:T(128)}, f32[2]{0:T(128)}) custom-call(s32[2]{0:T(128)S(1)} %and_select_fusion.mate_ref, f32[8,128]{1,0:T(8,128)S(1)} %get-tuple-element.23.dets_ref, f32[8,136,128]{2,1,0:T(8,128)} %get-tuple-element.20.own_ref, f32[8,136,128]{2,1,0:T(8,128)S(1)} %all-to-all-done.1.mate0_ref.mate1_ref, ...), custom_call_target="tpu_custom_call" | custom-call | flops 1 | bytes 1 | tf_op jit(solution)/shard_map/pallas_call | solution.py:390
  113.2 4.7 %all-to-all-done.2.table_ref = f32[256,1,128]{2,1,0:T(1,128)S(1)} async-done(((f32[256,1,128]{2,1,0:T(1,128)}), f32[256,1,128]{2,1,0:T(1,128)S(1)}, u32[]{:S(2)}, u32[]{:S(2)}) %all-to-all-start.2) | async-done | bytes 131104 | tf_op jit(solution)/shard_map/all_to_all | solution.py:457
  117.9 0.0 copy-done
  117.9 1.1 shard_map.70
  (1 shorter events, 0.0 us)
Async XLA Ops:
  9.2 15.7 %copy-start.1 = (f32[64]{0:T(128)S(1)}, f32[64]{0:T(128)}, u32[]{:S(2)}) copy-start(f32[64]{0:T(128)} %param.6) | copy-start | bytes 772
  9.2 70.0 %all-to-all-start = ((bf16[256,32,128]{2,1,0:T(8,128)(2,1)}), bf16[256,32,128]{2,1,0:T(8,128)(2,1)S(1)}, u32[]{:S(2)}, u32[]{:S(2)}) async-start(bf16[256,32,128]{2,1,0:T(8,128)(2,1)} %bitcast.4), calls=%async_computation | async-start | bytes 4194304 | tf_op jit(solution)/shard_map/all_to_all | solution.py:449
  83.1 13.8 %all-to-all-start.1 = ((f32[8,136,128]{2,1,0:T(8,128)}), f32[8,136,128]{2,1,0:T(8,128)S(1)}, u32[]{:S(2)}, u32[]{:S(2)}) async-start(f32[8,136,128]{2,1,0:T(8,128)} %get-tuple-element.20.own_ref), calls=%async_computation.1 | async-start | bytes 1114112 | tf_op jit(solution)/shard_map/all_to_all | solution.py:454
  86.6 18.3 %copy-start.2 = (s32[2]{0:T(128)S(1)}, s32[2]{0:T(128)}, u32[]{:S(2)}) copy-start(s32[2]{0:T(128)} %param.7) | copy-start | bytes 28
  86.6 31.3 %copy-start = (s32[32,128]{1,0:T(8,128)S(1)}, s32[32,128]{1,0:T(8,128)}, u32[]{:S(2)}) copy-start(s32[32,128]{1,0:T(8,128)} %get-tuple-element.22.target_ref) | copy-start | bytes 49156
  96.9 21.0 %all-to-all-start.2 = ((f32[256,1,128]{2,1,0:T(1,128)}), f32[256,1,128]{2,1,0:T(1,128)S(1)}, u32[]{:S(2)}, u32[]{:S(2)}) async-start(f32[256,1,128]{2,1,0:T(1,128)} %bitcast.2), calls=%async_computation.2 | async-start | bytes 262144 | tf_op jit(solution)/shard_map/all_to_all | solution.py:457
where the time goes:
time: 119 us
  waiting for transfers between devices  58.9 us (49%)
  Pallas kernels  32 us (27%)
  starting transfers between devices  27.2 us (23%)
    all_to_all x1, waiting for transfers between devices, shards(): lax.all_to_all(outgoing.reshape(devices, chunk, D), axes, split_axis=0, c...  54.2 us
    all_to_all x1, starting transfers between devices, shards(): lax.all_to_all(outgoing.reshape(devices, chunk, D), axes, split_axis=0, c...  15.7 us
    pallas_call x1, Pallas kernels, judge(): pl.pallas_call(judge_kernel, out_shape=(jax.ShapeDtypeStruct((depth // 16...  10.3 us
    pallas_call x1, Pallas kernels, dispatch(): pl.pallas_call(dispatch_kernel, out_shape=(jax.ShapeDtypeStruct(labels.sh...  8.59 us
    pallas_call x1, Pallas kernels, merge(): pl.pallas_call(merge_kernel, out_shape=(one, one), grid_spec=pltpu.Prefet...  8.29 us
    all_to_all x1, starting transfers between devices, shards(): lax.all_to_all(odds.reshape(devices, 1, 128), axes, split_axis=0, concat_...  8 us
    all_to_all x1, waiting for transfers between devices, shards(): lax.all_to_all(odds.reshape(devices, 1, 128), axes, split_axis=0, concat_...  4.71 us
    pallas_call x1, Pallas kernels, find_moments(): pl.pallas_call(moments_kernel, out_shape=(jax.ShapeDtypeStruct((FAR, D, d...  3.82 us
  transfers between devices with their start and end apart: 3, of which 2 were waited for; matrix products, arithmetic and copies ran while one was open for 0% of the time, Pallas kernels for 16%

commit v1 on v0

--- a/solution.py
+++ b/solution.py
@@ -15,7 +15,6 @@
 MERGE_FLOPS = 1
 FAR = 8
 NARROW_LIMIT = 16 * 1024 * 1024
-PANEL = 16
 STEP = 4
 PIECES = 4
 
@@ -32,14 +31,13 @@
     return high, middle, low
 
 
-def slots_of(labels):
+def slots_of(labels, emit):
     blocks = labels.shape[0]
     flipped = jnp.transpose(labels.astype(jnp.float32))
     before = iota((128, 128), 0) < iota((128, 128), 1)
     lanes = iota((128, 128), 1)
     levels = iota((8, 128), 0)
     running = jnp.zeros((8, 128), jnp.float32)
-    rows = []
     for b in range(blocks):
         across = labels[b : b + 1, :]
         down = jnp.broadcast_to(flipped[:, b : b + 1], (128, 128)).astype(jnp.int32)
@@ -49,11 +47,10 @@
         upper = levels == (across >> 7)
         found = jnp.take_along_axis(running, jnp.broadcast_to(low, (8, 128)), axis=1)
         earlier = jnp.sum(jnp.where(upper, found, 0.0), axis=0, keepdims=True)
-        rows.append(across * CAP + (inside + earlier).astype(jnp.int32))
+        emit(b, across * CAP + (inside + earlier).astype(jnp.int32))
         hot_low = jnp.where((down & 127) == lanes, 1.0, 0.0).astype(jnp.bfloat16)
         hot_up = jnp.where(upper, 1.0, 0.0).astype(jnp.bfloat16)
         running = running + jnp.dot(hot_up, hot_low, preferred_element_type=jnp.float32)
-    return jnp.concatenate(rows, axis=0)
 
 
 def dispatch_kernel(labels_ref, rows_ref, target_ref, out_ref, held, rows, wide, table, ready, places, sems):
@@ -63,25 +60,38 @@
     load_rows.start()
     table[...] = jnp.full(table.shape, EMPTY, jnp.float32)
     load_labels.wait()
-    target_ref[...] = slots_of(held[...])
-    copy = pltpu.make_async_copy(target_ref, places, sems.at[2])
-    copy.start()
+    blocks = held.shape[0]
+    half = blocks // 2
+    copies = [
+        pltpu.make_async_copy(
+            target_ref.at[pl.ds(k * half, half)], places.at[pl.ds(k * half, half)], sems.at[2 + k]
+        )
+        for k in range(2)
+    ]
+
+    def emit(b, line):
+        target_ref[b : b + 1, :] = line
+        if (b + 1) % half == 0:
+            copies[b // half].start()
+
+    slots_of(held[...], emit)
     load_rows.wait()
     wide[...] = rows[...].astype(jnp.float32)
-    copy.wait()
 
     def block(b, carry):
         for j in range(128):
             table[pl.ds(places[b, j], 1), :] = wide[pl.ds(b * 128 + j, 1), :]
         return carry
 
-    lax.fori_loop(0, held.shape[0], block, 0)
+    for k in range(2):
+        copies[k].wait()
+        lax.fori_loop(k * half, (k + 1) * half, block, 0)
     piece = table.shape[0] // PIECES
     stores = []
     for k in range(PIECES):
         part = pl.ds(k * piece, piece)
         ready[part, :] = table[part, :].astype(jnp.bfloat16)
-        stores.append(pltpu.make_async_copy(ready.at[part], out_ref.at[part], sems.at[3 + k]))
+        stores.append(pltpu.make_async_copy(ready.at[part], out_ref.at[part], sems.at[4 + k]))
         stores[-1].start()
     for store in stores:
         store.wait()
@@ -107,27 +117,27 @@
             pltpu.VMEM((slots, D), jnp.float32),
             pltpu.VMEM((slots, D), jnp.bfloat16),
             pltpu.SMEM(labels.shape, jnp.int32),
-            pltpu.SemaphoreType.DMA((3 + PIECES,)),
+            pltpu.SemaphoreType.DMA((4 + PIECES,)),
         ],
         compiler_params=pltpu.CompilerParams(vmem_limit_bytes=WIDE_LIMIT),
     )(labels, embedding)
 
 
-def eliminate(work, count):
+def eliminate(work, count, panel):
     pivots = [[] for _ in range(count)]
-    lanes = iota((PANEL, D), 1)
-    down = iota((PANEL, D), 0)
-    for p in range(D // PANEL):
-        base = p * PANEL
-        tiles = [work[m, base : base + PANEL, :] for m in range(count)]
-        diag = [jnp.ones((PANEL, D), jnp.float32) for _ in range(count)]
-        for i in range(0, PANEL, STEP):
+    lanes = iota((panel, D), 1)
+    down = iota((panel, D), 0)
+    for p in range(D // panel):
+        base = p * panel
+        tiles = [work[m, base : base + panel, :] for m in range(count)]
+        diag = [jnp.ones((panel, D), jnp.float32) for _ in range(count)]
+        for i in range(0, panel, STEP):
             inside = (lanes >= base + i) & (lanes < base + i + STEP)
             unit = jnp.where(lanes - base == down, 1.0, 0.0)
             for m in range(count):
                 tile = tiles[m]
                 columns = [
-                    jnp.broadcast_to(tile[:, base + i + t : base + i + t + 1], (PANEL, D))
+                    jnp.broadcast_to(tile[:, base + i + t : base + i + t + 1], (panel, D))
                     for t in range(STEP)
                 ]
                 small = [
@@ -149,8 +159,8 @@
                 tiles[m] = tile
         for m in range(count):
             pivots[m].append(diag[m])
-            work[m, base : base + PANEL, :] = tiles[m]
-            below = base + PANEL
+            work[m, base : base + panel, :] = tiles[m]
+            below = base + panel
             if below < D:
                 e1, e2, e3 = split3(tiles[m])
                 n1, n2, n3 = split3(tiles[m] * (1.0 / diag[m]))
@@ -187,10 +197,13 @@
     depth = rows_ref.shape[0] * 16
     moments = []
     for c in range(2):
-        rows = rows_ref[:, 16 * c : 16 * c + 16, :].reshape(depth, D)
-        empty = rows.astype(jnp.float32) > 8.0
-        clean = jnp.where(empty, 0.0, rows.astype(jnp.float32)).astype(jnp.bfloat16)
-        valid = jnp.where(empty, 0.0, 1.0).astype(jnp.bfloat16)
+        rows = rows_ref[:, 16 * c : 16 * c + 16, :]
+        wide = rows.astype(jnp.float32)
+        empty = wide > 8.0
+        wide = jnp.where(empty, 0.0, wide)
+        first_tile = jnp.sum(wide, axis=0)
+        number_tile = jnp.sum(jnp.where(empty, 0.0, 1.0), axis=0)
+        clean = wide.astype(jnp.bfloat16).reshape(depth, D)
         turned = jnp.transpose(clean)
         turned_ref[c] = turned
         stores.append(pltpu.make_async_copy(turned_ref.at[c], xt_ref.at[c], sems.at[c]))
@@ -201,13 +214,11 @@
             [jnp.where(zero_side, turned, none), jnp.where(zero_side, none, turned)], axis=0
         )
         second = jnp.dot(left, clean, preferred_element_type=jnp.float32)
-        side = ((iota((16, depth), 1) >> 3) & 1) == (iota((16, depth), 0) & 1)
-        pick = jnp.where(side, 1.0, 0.0).astype(jnp.bfloat16)
-        first = jnp.dot(pick, clean, preferred_element_type=jnp.float32)
-        number = jnp.dot(pick, valid, preferred_element_type=jnp.float32)
+        first = [jnp.sum(first_tile[8 * k : 8 * k + 8], axis=0, keepdims=True) for k in range(2)]
+        number = [jnp.sum(number_tile[8 * k : 8 * k + 8], axis=0, keepdims=True) for k in range(2)]
         for s in range(2):
             m = 2 * c + s
-            moments.append((second[s * D : (s + 1) * D], first[s : s + 1], number[s : s + 1]))
+            moments.append((second[s * D : (s + 1) * D], first[s], number[s]))
             second_ref[m] = moments[m][0]
     info_ref[...] = jnp.concatenate(
         [moments[m][1] for m in range(4)] + [moments[m][2] for m in range(4)], axis=0
@@ -259,7 +270,7 @@
     numbers = [info_ref[m : m + 1, :] for m in range(4, 8)]
     for m in range(4):
         work[m] = posterior_scatter(second_ref[m], firsts[m], numbers[m])
-    pivots = eliminate(work, 4)
+    pivots = eliminate(work, 4, 32)
     logdets = [log_sum(tiles) for tiles in pivots]
     dets_ref[...] = jnp.concatenate(logdets + numbers, axis=0)
     lower = iota((D, D), 0) >= iota((D, D), 1)
@@ -371,7 +382,7 @@
     stats = own + mates + both
     for m in range(6):
         work[m] = posterior_scatter(*stats[m])
-    pivots = eliminate(work, 6)
+    pivots = eliminate(work, 6, 16)
     blank = [jnp.ones((6, D), jnp.float32)]
     numbers = jnp.concatenate([dets_ref[4:8, :]] + [stats[m][2] for m in range(6)] + blank, axis=0)
     logdets = jnp.concatenate([dets_ref[0:4, :]] + [log_sum(pivots[m]) for m in range(6)] + blank, axis=0)

time: 119 us -> 119 us (level)
  no operation moved by 1% of the time
where the time goes in v1:
time: 119 us; the launch traced here: 118 us
  waiting for transfers between devices  58.9 us (49%)
  Pallas kernels  31.5 us (26%)
  starting transfers between devices  27.2 us (23%)
    all_to_all x1, waiting for transfers between devices, shards(): lax.all_to_all(outgoing.reshape(devices, chunk, D), axes, split_axis=0, c...  54.2 us
    all_to_all x1, starting transfers between devices, shards(): lax.all_to_all(outgoing.reshape(devices, chunk, D), axes, split_axis=0, c...  15.7 us
    pallas_call x1, Pallas kernels, judge(): pl.pallas_call(judge_kernel, out_shape=(jax.ShapeDtypeStruct((depth // 16...  10.4 us
    pallas_call x1, Pallas kernels, merge(): pl.pallas_call(merge_kernel, out_shape=(one, one), grid_spec=pltpu.Prefet...  8.29 us
    pallas_call x1, Pallas kernels, dispatch(): pl.pallas_call(dispatch_kernel, out_shape=(jax.ShapeDtypeStruct(labels.sh...  7.95 us
    all_to_all x1, starting transfers between devices, shards(): lax.all_to_all(odds.reshape(devices, 1, 128), axes, split_axis=0, concat_...  7.82 us
    all_to_all x1, waiting for transfers between devices, shards(): lax.all_to_all(odds.reshape(devices, 1, 128), axes, split_axis=0, concat_...  4.69 us
    pallas_call x1, Pallas kernels, find_moments(): pl.pallas_call(moments_kernel, out_shape=(jax.ShapeDtypeStruct((FAR, D, d...  3.72 us
  transfers between devices with their start and end apart: 3, of which 2 were waited for; matrix products, arithmetic and copies ran while one was open for 0% of the time, Pallas kernels for 16%

profile of v1, /device:TPU:1, one launch (start us, length us, event | category | flops | bytes accessed | tf_op | source)
XLA Modules:
  0.0 118.4 jit_solution(11544053676316134935)
XLA Ops:
  0.6 7.9 %shard_map.67 = (s32[32,128]{1,0:T(8,128)}, bf16[8192,128]{1,0:T(8,128)(2,1)}) custom-call(s32[32,128]{1,0:T(8,128)} %bitcast.5, bf16[4096,128]{1,0:T(8,128)(2,1)} %rows_ref.1), custom_call_target="tpu_custom_call" | custom-call | tf_op jit(solution)/shard_map/pallas_call | solution.py:102
  8.6 0.0 copy-start.1
  8.6 15.7 %all-to-all-start = ((bf16[256,32,128]{2,1,0:T(8,128)(2,1)}), bf16[256,32,128]{2,1,0:T(8,128)(2,1)S(1)}, u32[]{:S(2)}, u32[]{:S(2)}) async-start(bf16[256,32,128]{2,1,0:T(8,128)(2,1)} %bitcast.4), calls=%async_computation | async-start | bytes 4194304 | tf_op jit(solution)/shard_map/all_to_all | solution.py:460
  24.3 0.0 copy-done.1
  24.3 0.1 dynamic_slice.3.logit_ref
  24.4 54.2 %all-to-all-done.rows_ref = bf16[256,32,128]{2,1,0:T(8,128)(2,1)S(1)} async-done(((bf16[256,32,128]{2,1,0:T(8,128)(2,1)}), bf16[256,32,128]{2,1,0:T(8,128)(2,1)S(1)}, u32[]{:S(2)}, u32[]{:S(2)}) %all-to-all-start) | async-done | bytes 2097184 | tf_op jit(solution)/shard_map/all_to_all | solution.py:460
  78.6 3.7 %shard_map.68 = (bf16[8,128,4096]{2,1,0:T(8,128)(2,1)}, f32[4,128,128]{2,1,0:T(8,128)S(1)}, f32[8,128]{1,0:T(8,128)S(1)}, f32[8,136,128]{2,1,0:T(8,128)}) custom-call(bf16[256,32,128]{2,1,0:T(8,128)(2,1)S(1)} %all-to-all-done.rows_ref), custom_call_target="tpu_custom_call" | custom-call | flops 1000000000 | bytes 4000000 | tf_op jit(solution)/shard_map/pallas_call | solution.py:245
  82.3 3.7 %all-to-all-start.1 = ((f32[8,136,128]{2,1,0:T(8,128)}), f32[8,136,128]{2,1,0:T(8,128)S(1)}, u32[]{:S(2)}, u32[]{:S(2)}) async-start(f32[8,136,128]{2,1,0:T(8,128)} %get-tuple-element.20.own_ref), calls=%async_computation.1 | async-start | bytes 1114112 | tf_op jit(solution)/shard_map/all_to_all | solution.py:465
  86.0 0.0 copy-start.2
  86.0 0.0 copy-start
  86.0 10.4 %shard_map.69 = (f32[256,128]{1,0:T(8,128)}, f32[8,128]{1,0:T(8,128)S(1)}) custom-call(f32[2]{0:T(128)S(1)} %dynamic_slice.3.logit_ref, bf16[8,128,4096]{2,1,0:T(8,128)(2,1)} %get-tuple-element.16.far_ref, f32[4,128,128]{2,1,0:T(8,128)S(1)} %get-tuple-element.17.second_ref, f32[8,128]{1,0:T(8,128)S(1)} %get-tuple-element.18.info_ref), custom_call_target="tpu_custom_call" | custom-call | flops 10000000000 | bytes 10000000 | tf_op jit(solution)/shard_map/pallas_call | solution.py:317
  96.5 0.0 all-to-all-done.1.mate0_ref.mate1_ref
  96.5 7.8 %all-to-all-start.2 = ((f32[256,1,128]{2,1,0:T(1,128)}), f32[256,1,128]{2,1,0:T(1,128)S(1)}, u32[]{:S(2)}, u32[]{:S(2)}) async-start(f32[256,1,128]{2,1,0:T(1,128)} %bitcast.2), calls=%async_computation.2 | async-start | bytes 262144 | tf_op jit(solution)/shard_map/all_to_all | solution.py:468
  104.3 0.0 copy-done.2
  104.3 8.3 %shard_map.71 = (f32[2]{0:T(128)}, f32[2]{0:T(128)}) custom-call(s32[2]{0:T(128)S(1)} %and_select_fusion.mate_ref, f32[8,128]{1,0:T(8,128)S(1)} %get-tuple-element.23.dets_ref, f32[8,136,128]{2,1,0:T(8,128)} %get-tuple-element.20.own_ref, f32[8,136,128]{2,1,0:T(8,128)S(1)} %all-to-all-done.1.mate0_ref.mate1_ref, ...), custom_call_target="tpu_custom_call" | custom-call | flops 1 | bytes 1 | tf_op jit(solution)/shard_map/pallas_call | solution.py:401
  112.6 4.7 %all-to-all-done.2.table_ref = f32[256,1,128]{2,1,0:T(1,128)S(1)} async-done(((f32[256,1,128]{2,1,0:T(1,128)}), f32[256,1,128]{2,1,0:T(1,128)S(1)}, u32[]{:S(2)}, u32[]{:S(2)}) %all-to-all-start.2) | async-done | bytes 131104 | tf_op jit(solution)/shard_map/all_to_all | solution.py:468
  117.3 0.0 copy-done
  117.3 1.1 shard_map.70
  (1 shorter events, 0.0 us)
Async XLA Ops:
  8.6 15.7 %copy-start.1 = (f32[64]{0:T(128)S(1)}, f32[64]{0:T(128)}, u32[]{:S(2)}) copy-start(f32[64]{0:T(128)} %param.6) | copy-start | bytes 772
  8.6 70.0 %all-to-all-start = ((bf16[256,32,128]{2,1,0:T(8,128)(2,1)}), bf16[256,32,128]{2,1,0:T(8,128)(2,1)S(1)}, u32[]{:S(2)}, u32[]{:S(2)}) async-start(bf16[256,32,128]{2,1,0:T(8,128)(2,1)} %bitcast.4), calls=%async_computation | async-start | bytes 4194304 | tf_op jit(solution)/shard_map/all_to_all | solution.py:460
  82.3 14.2 %all-to-all-start.1 = ((f32[8,136,128]{2,1,0:T(8,128)}), f32[8,136,128]{2,1,0:T(8,128)S(1)}, u32[]{:S(2)}, u32[]{:S(2)}) async-start(f32[8,136,128]{2,1,0:T(8,128)} %get-tuple-element.20.own_ref), calls=%async_computation.1 | async-start | bytes 1114112 | tf_op jit(solution)/shard_map/all_to_all | solution.py:465
  86.0 18.3 %copy-start.2 = (s32[2]{0:T(128)S(1)}, s32[2]{0:T(128)}, u32[]{:S(2)}) copy-start(s32[2]{0:T(128)} %param.7) | copy-start | bytes 28
  86.0 31.3 %copy-start = (s32[32,128]{1,0:T(8,128)S(1)}, s32[32,128]{1,0:T(8,128)}, u32[]{:S(2)}) copy-start(s32[32,128]{1,0:T(8,128)} %get-tuple-element.22.target_ref) | copy-start | bytes 49156
  96.5 20.8 %all-to-all-start.2 = ((f32[256,1,128]{2,1,0:T(1,128)}), f32[256,1,128]{2,1,0:T(1,128)S(1)}, u32[]{:S(2)}, u32[]{:S(2)}) async-start(f32[256,1,128]{2,1,0:T(1,128)} %bitcast.2), calls=%async_computation.2 | async-start | bytes 262144 | tf_op jit(solution)/shard_map/all_to_all | solution.py:468

commit v2 on v1

--- a/solution.py
+++ b/solution.py
@@ -13,7 +13,7 @@
 VMEM_LIMIT = 48 * 1024 * 1024
 WIDE_LIMIT = 60 * 1024 * 1024
 MERGE_FLOPS = 1
-FAR = 8
+FAR = 4
 NARROW_LIMIT = 16 * 1024 * 1024
 STEP = 4
 PIECES = 4
@@ -188,13 +188,15 @@
 
 def posterior_scatter(second, first, number):
     same = iota((D, D), 0) == iota((D, D), 1)
-    over = jnp.broadcast_to(first, (D, D))
-    return jnp.where(same, 1.0, 0.0) + second - jnp.transpose(over) * over / (1.0 + number)
-
-
-def moments_kernel(rows_ref, xt_ref, second_ref, info_ref, pack_ref, turned_ref, sems):
-    stores = []
-    depth = rows_ref.shape[0] * 16
+    column = jnp.transpose(jnp.broadcast_to(first, (8, D)))[:, 0:1]
+    return jnp.where(same, 1.0, 0.0) + second - column * first / (1.0 + number)
+
+
+def moments_kernel(rows_ref, far_ref, second_ref, info_ref, pack_ref, sem):
+    sources = rows_ref.shape[0]
+    keep = pltpu.make_async_copy(rows_ref, far_ref.at[pl.ds(0, sources)], sem)
+    keep.start()
+    depth = sources * 16
     moments = []
     for c in range(2):
         rows = rows_ref[:, 16 * c : 16 * c + 16, :]
@@ -205,9 +207,6 @@
         number_tile = jnp.sum(jnp.where(empty, 0.0, 1.0), axis=0)
         clean = wide.astype(jnp.bfloat16).reshape(depth, D)
         turned = jnp.transpose(clean)
-        turned_ref[c] = turned
-        stores.append(pltpu.make_async_copy(turned_ref.at[c], xt_ref.at[c], sems.at[c]))
-        stores[c].start()
         zero_side = (iota((D, depth), 1) & 8) == 0
         none = jnp.zeros_like(turned)
         left = jnp.concatenate(
@@ -235,17 +234,16 @@
     for q in range(pack_ref.shape[0]):
         pack_ref[q, 0:D, :] = packed
         pack_ref[q, D : D + 8, :] = ending
-    for store in stores:
-        store.wait()
+    keep.wait()
 
 
 def find_moments(arrived, owners):
-    depth = arrived.shape[0] * 16
+    sources, chunk, _ = arrived.shape
     f32 = jnp.float32
     return pl.pallas_call(
         moments_kernel,
         out_shape=(
-            jax.ShapeDtypeStruct((FAR, D, depth), jnp.bfloat16),
+            jax.ShapeDtypeStruct((FAR * sources, chunk, D), jnp.bfloat16),
             jax.ShapeDtypeStruct((4, D, D), f32),
             jax.ShapeDtypeStruct((8, D), f32),
             jax.ShapeDtypeStruct((owners, D + 8, D), f32),
@@ -253,19 +251,17 @@
         in_specs=[pl.BlockSpec(memory_space=pltpu.VMEM)],
         out_specs=[pl.BlockSpec(memory_space=pltpu.HBM)]
         + [pl.BlockSpec(memory_space=pltpu.VMEM)] * 3,
-        scratch_shapes=[
-            pltpu.VMEM((2, D, depth), jnp.bfloat16),
-            pltpu.SemaphoreType.DMA((2,)),
-        ],
+        scratch_shapes=[pltpu.SemaphoreType.DMA],
         compiler_params=pltpu.CompilerParams(vmem_limit_bytes=VMEM_LIMIT),
         cost_estimate=pl.CostEstimate(flops=10**9, bytes_accessed=4 * 10**6, transcendentals=0),
     )(arrived)
 
 
-def judge_kernel(logit_ref, far_ref, second_ref, info_ref, odds_ref, dets_ref, work, lines, xt_ref, sem):
-    load = pltpu.make_async_copy(far_ref.at[0:2], xt_ref, sem)
+def judge_kernel(logit_ref, far_ref, second_ref, info_ref, odds_ref, dets_ref, work, lines, rows_ref, sem):
+    sources = rows_ref.shape[0]
+    load = pltpu.make_async_copy(far_ref.at[pl.ds(0, sources)], rows_ref, sem)
     load.start()
-    clusters, _, depth = xt_ref.shape
+    clusters, depth = 2, sources * 16
     firsts = [info_ref[m : m + 1, :] for m in range(4)]
     numbers = [info_ref[m : m + 1, :] for m in range(4, 8)]
     for m in range(4):
@@ -294,9 +290,13 @@
         shift = jnp.concatenate(shifts, axis=0)
         base = logit_ref[c] + (offsets[1] - offsets[0])
         for w in range(depth // width):
-            columns = xt_ref[c, :, w * width : (w + 1) * width]
-            image = jnp.dot(
-                maps, jnp.concatenate([columns] * 3, axis=0), preferred_element_type=jnp.float32
+            part = slice(w * (width // 16), (w + 1) * (width // 16))
+            rows = rows_ref[part, 16 * c : 16 * c + 16, :].reshape(width, D)
+            image = lax.dot_general(
+                maps,
+                jnp.concatenate([rows] * 3, axis=1),
+                (((1,), (1,)), ((), ())),
+                preferred_element_type=jnp.float32,
             )
             image = image - shift
             squares = image * image
@@ -311,13 +311,13 @@
         odds_ref[pl.ds(s, depth // 128, stride=8), :] = jnp.where(lanes < 16, first, second)
 
 
-def judge(logits, xt, second, info):
-    depth = xt.shape[2]
+def judge(logits, far, second, info):
+    sources, chunk = far.shape[0] // FAR, far.shape[1]
     f32 = jnp.float32
     return pl.pallas_call(
         judge_kernel,
         out_shape=(
-            jax.ShapeDtypeStruct((depth // 16, 128), f32),
+            jax.ShapeDtypeStruct((sources, 128), f32),
             jax.ShapeDtypeStruct((8, D), f32),
         ),
         in_specs=[
@@ -329,13 +329,13 @@
         out_specs=[pl.BlockSpec(memory_space=pltpu.VMEM)] * 2,
         scratch_shapes=[
             pltpu.VMEM((4, D, D), f32),
-            pltpu.VMEM((depth // 128, 128), f32),
-            pltpu.VMEM((2, D, depth), jnp.bfloat16),
+            pltpu.VMEM((sources // 8, 128), f32),
+            pltpu.VMEM((sources, chunk, D), jnp.bfloat16),
             pltpu.SemaphoreType.DMA,
         ],
         compiler_params=pltpu.CompilerParams(vmem_limit_bytes=VMEM_LIMIT),
         cost_estimate=pl.CostEstimate(flops=10**10, bytes_accessed=10**7, transcendentals=0),
-    )(logits, xt, second, info)
+    )(logits, far, second, info)
 
 
 def unpack(pack):
@@ -461,9 +461,9 @@
         outgoing.reshape(devices, chunk, D), axes, split_axis=0, concat_axis=0, tiled=True
     )
     logits = lax.dynamic_slice(sub_logit, (lax.axis_index("rows") * per_holder,), (per_holder,))
-    xt, second, info, packs = find_moments(arrived, owners)
+    far, second, info, packs = find_moments(arrived, owners)
     everyone = lax.all_to_all(packs, "own", split_axis=0, concat_axis=0, tiled=True)
-    odds, dets = judge(logits, xt, second, info)
+    odds, dets = judge(logits, far, second, info)
     odds, everyone = lax.optimization_barrier((odds, everyone))
     returned = lax.all_to_all(
         odds.reshape(devices, 1, 128), axes, split_axis=0, concat_axis=0, tiled=True

time: 119 us -> 118 us (level)
  no operation moved by 1% of the time
where the time goes in v2:
time: 118 us
  waiting for transfers between devices  58.6 us (50%)
  Pallas kernels  31 us (26%)
  starting transfers between devices  27.1 us (23%)
    all_to_all x1, waiting for transfers between devices, shards(): lax.all_to_all(outgoing.reshape(devices, chunk, D), axes, split_axis=0, c...  54.2 us
    all_to_all x1, starting transfers between devices, shards(): lax.all_to_all(outgoing.reshape(devices, chunk, D), axes, split_axis=0, c...  15.7 us
    pallas_call x1, Pallas kernels, judge(): pl.pallas_call(judge_kernel, out_shape=(jax.ShapeDtypeStruct((sources, 12...  10.6 us
    pallas_call x1, Pallas kernels, merge(): pl.pallas_call(merge_kernel, out_shape=(one, one), grid_spec=pltpu.Prefet...  8.62 us
    all_to_all x1, starting transfers between devices, shards(): lax.all_to_all(odds.reshape(devices, 1, 128), axes, split_axis=0, concat_...  7.97 us
    pallas_call x1, Pallas kernels, dispatch(): pl.pallas_call(dispatch_kernel, out_shape=(jax.ShapeDtypeStruct(labels.sh...  7.95 us
    all_to_all x1, waiting for transfers between devices, shards(): lax.all_to_all(odds.reshape(devices, 1, 128), axes, split_axis=0, concat_...  4.37 us
    all_to_all x1, starting transfers between devices, shards(): lax.all_to_all(packs, 'own', split_axis=0, concat_axis=0, tiled=True)  3.5 us
  transfers between devices with their start and end apart: 3, of which 2 were waited for; matrix products, arithmetic and copies ran while one was open for 0% of the time, Pallas kernels for 16%

profile of v2, /device:TPU:1, one launch (start us, length us, event | category | flops | bytes accessed | tf_op | source)
XLA Modules:
  0.0 117.5 jit_solution(468706737389960237)
XLA Ops:
  0.6 7.9 %shard_map.67 = (s32[32,128]{1,0:T(8,128)}, bf16[8192,128]{1,0:T(8,128)(2,1)}) custom-call(s32[32,128]{1,0:T(8,128)} %bitcast.5, bf16[4096,128]{1,0:T(8,128)(2,1)} %rows_ref.1), custom_call_target="tpu_custom_call" | custom-call | tf_op jit(solution)/shard_map/pallas_call | solution.py:102
  8.6 0.0 copy-start.1
  8.6 15.7 %all-to-all-start = ((bf16[256,32,128]{2,1,0:T(8,128)(2,1)}), bf16[256,32,128]{2,1,0:T(8,128)(2,1)S(1)}, u32[]{:S(2)}, u32[]{:S(2)}) async-start(bf16[256,32,128]{2,1,0:T(8,128)(2,1)} %bitcast.4), calls=%async_computation | async-start | bytes 4194304 | tf_op jit(solution)/shard_map/all_to_all | solution.py:460
  24.3 0.0 copy-done.1
  24.3 0.1 dynamic_slice.3.logit_ref
  24.4 54.2 %all-to-all-done.rows_ref = bf16[256,32,128]{2,1,0:T(8,128)(2,1)S(1)} async-done(((bf16[256,32,128]{2,1,0:T(8,128)(2,1)}), bf16[256,32,128]{2,1,0:T(8,128)(2,1)S(1)}, u32[]{:S(2)}, u32[]{:S(2)}) %all-to-all-start) | async-done | bytes 2097184 | tf_op jit(solution)/shard_map/all_to_all | solution.py:460
  78.6 2.7 %shard_map.68 = (bf16[1024,32,128]{2,1,0:T(8,128)(2,1)}, f32[4,128,128]{2,1,0:T(8,128)S(1)}, f32[8,128]{1,0:T(8,128)S(1)}, f32[8,136,128]{2,1,0:T(8,128)}) custom-call(bf16[256,32,128]{2,1,0:T(8,128)(2,1)S(1)} %all-to-all-done.rows_ref), custom_call_target="tpu_custom_call" | custom-call | flops 1000000000 | bytes 4000000 | tf_op jit(solution)/shard_map/pallas_call | solution.py:243
  81.3 3.5 %all-to-all-start.1 = ((f32[8,136,128]{2,1,0:T(8,128)}), f32[8,136,128]{2,1,0:T(8,128)S(1)}, u32[]{:S(2)}, u32[]{:S(2)}) async-start(f32[8,136,128]{2,1,0:T(8,128)} %get-tuple-element.20.own_ref), calls=%async_computation.1 | async-start | bytes 1114112 | tf_op jit(solution)/shard_map/all_to_all | solution.py:465
  84.8 0.0 copy-start.2
  84.8 0.0 copy-start
  84.9 10.6 %shard_map.69 = (f32[256,128]{1,0:T(8,128)}, f32[8,128]{1,0:T(8,128)S(1)}) custom-call(f32[2]{0:T(128)S(1)} %dynamic_slice.3.logit_ref, bf16[1024,32,128]{2,1,0:T(8,128)(2,1)} %get-tuple-element.16.far_ref, f32[4,128,128]{2,1,0:T(8,128)S(1)} %get-tuple-element.17.second_ref, f32[8,128]{1,0:T(8,128)S(1)} %get-tuple-element.18.info_ref), custom_call_target="tpu_custom_call" | custom-call | flops 10000000000 | bytes 10000000 | tf_op jit(solution)/shard_map/pallas_call | solution.py:317
  95.4 0.0 all-to-all-done.1.mate0_ref.mate1_ref
  95.5 8.0 %all-to-all-start.2 = ((f32[256,1,128]{2,1,0:T(1,128)}), f32[256,1,128]{2,1,0:T(1,128)S(1)}, u32[]{:S(2)}, u32[]{:S(2)}) async-start(f32[256,1,128]{2,1,0:T(1,128)} %bitcast.2), calls=%async_computation.2 | async-start | bytes 262144 | tf_op jit(solution)/shard_map/all_to_all | solution.py:468
  103.4 0.0 copy-done.2
  103.5 8.6 %shard_map.71 = (f32[2]{0:T(128)}, f32[2]{0:T(128)}) custom-call(s32[2]{0:T(128)S(1)} %and_select_fusion.mate_ref, f32[8,128]{1,0:T(8,128)S(1)} %get-tuple-element.23.dets_ref, f32[8,136,128]{2,1,0:T(8,128)} %get-tuple-element.20.own_ref, f32[8,136,128]{2,1,0:T(8,128)S(1)} %all-to-all-done.1.mate0_ref.mate1_ref, ...), custom_call_target="tpu_custom_call" | custom-call | flops 1 | bytes 1 | tf_op jit(solution)/shard_map/pallas_call | solution.py:401
  112.1 4.4 %all-to-all-done.2.table_ref = f32[256,1,128]{2,1,0:T(1,128)S(1)} async-done(((f32[256,1,128]{2,1,0:T(1,128)}), f32[256,1,128]{2,1,0:T(1,128)S(1)}, u32[]{:S(2)}, u32[]{:S(2)}) %all-to-all-start.2) | async-done | bytes 131104 | tf_op jit(solution)/shard_map/all_to_all | solution.py:468
  116.5 0.0 copy-done
  116.5 1.1 shard_map.70
  (1 shorter events, 0.0 us)
Async XLA Ops:
  8.6 15.7 %copy-start.1 = (f32[64]{0:T(128)S(1)}, f32[64]{0:T(128)}, u32[]{:S(2)}) copy-start(f32[64]{0:T(128)} %param.6) | copy-start | bytes 772
  8.6 70.0 %all-to-all-start = ((bf16[256,32,128]{2,1,0:T(8,128)(2,1)}), bf16[256,32,128]{2,1,0:T(8,128)(2,1)S(1)}, u32[]{:S(2)}, u32[]{:S(2)}) async-start(bf16[256,32,128]{2,1,0:T(8,128)(2,1)} %bitcast.4), calls=%async_computation | async-start | bytes 4194304 | tf_op jit(solution)/shard_map/all_to_all | solution.py:460
  81.3 14.1 %all-to-all-start.1 = ((f32[8,136,128]{2,1,0:T(8,128)}), f32[8,136,128]{2,1,0:T(8,128)S(1)}, u32[]{:S(2)}, u32[]{:S(2)}) async-start(f32[8,136,128]{2,1,0:T(8,128)} %get-tuple-element.20.own_ref), calls=%async_computation.1 | async-start | bytes 1114112 | tf_op jit(solution)/shard_map/all_to_all | solution.py:465
  84.8 18.6 %copy-start.2 = (s32[2]{0:T(128)S(1)}, s32[2]{0:T(128)}, u32[]{:S(2)}) copy-start(s32[2]{0:T(128)} %param.7) | copy-start | bytes 28
  84.8 31.6 %copy-start = (s32[32,128]{1,0:T(8,128)S(1)}, s32[32,128]{1,0:T(8,128)}, u32[]{:S(2)}) copy-start(s32[32,128]{1,0:T(8,128)} %get-tuple-element.22.target_ref) | copy-start | bytes 49156
  95.5 21.0 %all-to-all-start.2 = ((f32[256,1,128]{2,1,0:T(1,128)}), f32[256,1,128]{2,1,0:T(1,128)S(1)}, u32[]{:S(2)}, u32[]{:S(2)}) async-start(f32[256,1,128]{2,1,0:T(1,128)} %bitcast.2), calls=%async_computation.2 | async-start | bytes 262144 | tf_op jit(solution)/shard_map/all_to_all | solution.py:468

commit v3 on v2

--- a/solution.py
+++ b/solution.py
@@ -69,23 +69,26 @@
         for k in range(2)
     ]
 
+    load_rows.wait()
+    wide[...] = rows[...].astype(jnp.float32)
+
+    def block(b, carry):
+        for j in range(128):
+            table[pl.ds(places[b, j], 1), :] = wide[pl.ds(b * 128 + j, 1), :]
+        return carry
+
     def emit(b, line):
         target_ref[b : b + 1, :] = line
         if (b + 1) % half == 0:
             copies[b // half].start()
+        if b == half:
+            copies[0].wait()
+        if b >= half:
+            block(b - half, 0)
 
     slots_of(held[...], emit)
-    load_rows.wait()
-    wide[...] = rows[...].astype(jnp.float32)
-
-    def block(b, carry):
-        for j in range(128):
-            table[pl.ds(places[b, j], 1), :] = wide[pl.ds(b * 128 + j, 1), :]
-        return carry
-
-    for k in range(2):
-        copies[k].wait()
-        lax.fori_loop(k * half, (k + 1) * half, block, 0)
+    copies[1].wait()
+    lax.fori_loop(half, blocks, block, 0)
     piece = table.shape[0] // PIECES
     stores = []
     for k in range(PIECES):

time: 118 us -> 118 us (level)
  no operation moved by 1% of the time
where the time goes in v3:
time: 118 us
  waiting for transfers between devices  58.6 us (50%)
  Pallas kernels  31.2 us (26%)
  starting transfers between devices  27.2 us (23%)
    all_to_all x1, waiting for transfers between devices, shards(): lax.all_to_all(outgoing.reshape(devices, chunk, D), axes, split_axis=0, c...  54.2 us
    all_to_all x1, starting transfers between devices, shards(): lax.all_to_all(outgoing.reshape(devices, chunk, D), axes, split_axis=0, c...  15.7 us
    pallas_call x1, Pallas kernels, judge(): pl.pallas_call(judge_kernel, out_shape=(jax.ShapeDtypeStruct((sources, 12...  10.6 us
    pallas_call x1, Pallas kernels, merge(): pl.pallas_call(merge_kernel, out_shape=(one, one), grid_spec=pltpu.Prefet...  8.62 us
    pallas_call x1, Pallas kernels, dispatch(): pl.pallas_call(dispatch_kernel, out_shape=(jax.ShapeDtypeStruct(labels.sh...  8.25 us
    all_to_all x1, starting transfers between devices, shards(): lax.all_to_all(odds.reshape(devices, 1, 128), axes, split_axis=0, concat_...  7.82 us
    all_to_all x1, waiting for transfers between devices, shards(): lax.all_to_all(odds.reshape(devices, 1, 128), axes, split_axis=0, concat_...  4.36 us
    all_to_all x1, starting transfers between devices, shards(): lax.all_to_all(packs, 'own', split_axis=0, concat_axis=0, tiled=True)  3.68 us
  transfers between devices with their start and end apart: 3, of which 2 were waited for; matrix products, arithmetic and copies ran while one was open for 0% of the time, Pallas kernels for 16%

profile of v3, /device:TPU:1, one launch (start us, length us, event | category | flops | bytes accessed | tf_op | source)
XLA Modules:
  0.0 117.8 jit_solution(500112073493593268)
XLA Ops:
  0.6 8.2 %shard_map.67 = (s32[32,128]{1,0:T(8,128)}, bf16[8192,128]{1,0:T(8,128)(2,1)}) custom-call(s32[32,128]{1,0:T(8,128)} %bitcast.5, bf16[4096,128]{1,0:T(8,128)(2,1)} %rows_ref.1), custom_call_target="tpu_custom_call" | custom-call | tf_op jit(solution)/shard_map/pallas_call | solution.py:105
  8.9 0.0 copy-start.1
  8.9 15.7 %all-to-all-start = ((bf16[256,32,128]{2,1,0:T(8,128)(2,1)}), bf16[256,32,128]{2,1,0:T(8,128)(2,1)S(1)}, u32[]{:S(2)}, u32[]{:S(2)}) async-start(bf16[256,32,128]{2,1,0:T(8,128)(2,1)} %bitcast.4), calls=%async_computation | async-start | bytes 4194304 | tf_op jit(solution)/shard_map/all_to_all | solution.py:463
  24.6 0.0 copy-done.1
  24.6 0.1 dynamic_slice.3.logit_ref
  24.7 54.2 %all-to-all-done.rows_ref = bf16[256,32,128]{2,1,0:T(8,128)(2,1)S(1)} async-done(((bf16[256,32,128]{2,1,0:T(8,128)(2,1)}), bf16[256,32,128]{2,1,0:T(8,128)(2,1)S(1)}, u32[]{:S(2)}, u32[]{:S(2)}) %all-to-all-start) | async-done | bytes 2097184 | tf_op jit(solution)/shard_map/all_to_all | solution.py:463
  78.9 2.7 %shard_map.68 = (bf16[1024,32,128]{2,1,0:T(8,128)(2,1)}, f32[4,128,128]{2,1,0:T(8,128)S(1)}, f32[8,128]{1,0:T(8,128)S(1)}, f32[8,136,128]{2,1,0:T(8,128)}) custom-call(bf16[256,32,128]{2,1,0:T(8,128)(2,1)S(1)} %all-to-all-done.rows_ref), custom_call_target="tpu_custom_call" | custom-call | flops 1000000000 | bytes 4000000 | tf_op jit(solution)/shard_map/pallas_call | solution.py:246
  81.6 3.7 %all-to-all-start.1 = ((f32[8,136,128]{2,1,0:T(8,128)}), f32[8,136,128]{2,1,0:T(8,128)S(1)}, u32[]{:S(2)}, u32[]{:S(2)}) async-start(f32[8,136,128]{2,1,0:T(8,128)} %get-tuple-element.20.own_ref), calls=%async_computation.1 | async-start | bytes 1114112 | tf_op jit(solution)/shard_map/all_to_all | solution.py:468
  85.3 0.0 copy-start.2
  85.3 0.0 copy-start
  85.3 10.6 %shard_map.69 = (f32[256,128]{1,0:T(8,128)}, f32[8,128]{1,0:T(8,128)S(1)}) custom-call(f32[2]{0:T(128)S(1)} %dynamic_slice.3.logit_ref, bf16[1024,32,128]{2,1,0:T(8,128)(2,1)} %get-tuple-element.16.far_ref, f32[4,128,128]{2,1,0:T(8,128)S(1)} %get-tuple-element.17.second_ref, f32[8,128]{1,0:T(8,128)S(1)} %get-tuple-element.18.info_ref), custom_call_target="tpu_custom_call" | custom-call | flops 10000000000 | bytes 10000000 | tf_op jit(solution)/shard_map/pallas_call | solution.py:320
  95.9 0.0 all-to-all-done.1.mate0_ref.mate1_ref
  95.9 7.8 %all-to-all-start.2 = ((f32[256,1,128]{2,1,0:T(1,128)}), f32[256,1,128]{2,1,0:T(1,128)S(1)}, u32[]{:S(2)}, u32[]{:S(2)}) async-start(f32[256,1,128]{2,1,0:T(1,128)} %bitcast.2), calls=%async_computation.2 | async-start | bytes 262144 | tf_op jit(solution)/shard_map/all_to_all | solution.py:471
  103.8 0.0 copy-done.2
  103.8 8.6 %shard_map.71 = (f32[2]{0:T(128)}, f32[2]{0:T(128)}) custom-call(s32[2]{0:T(128)S(1)} %and_select_fusion.mate_ref, f32[8,128]{1,0:T(8,128)S(1)} %get-tuple-element.23.dets_ref, f32[8,136,128]{2,1,0:T(8,128)} %get-tuple-element.20.own_ref, f32[8,136,128]{2,1,0:T(8,128)S(1)} %all-to-all-done.1.mate0_ref.mate1_ref, ...), custom_call_target="tpu_custom_call" | custom-call | flops 1 | bytes 1 | tf_op jit(solution)/shard_map/pallas_call | solution.py:404
  112.4 4.4 %all-to-all-done.2.table_ref = f32[256,1,128]{2,1,0:T(1,128)S(1)} async-done(((f32[256,1,128]{2,1,0:T(1,128)}), f32[256,1,128]{2,1,0:T(1,128)S(1)}, u32[]{:S(2)}, u32[]{:S(2)}) %all-to-all-start.2) | async-done | bytes 131104 | tf_op jit(solution)/shard_map/all_to_all | solution.py:471
  116.8 0.0 copy-done
  116.8 1.1 shard_map.70
  (1 shorter events, 0.0 us)
Async XLA Ops:
  8.9 15.7 %copy-start.1 = (f32[64]{0:T(128)S(1)}, f32[64]{0:T(128)}, u32[]{:S(2)}) copy-start(f32[64]{0:T(128)} %param.6) | copy-start | bytes 772
  8.9 70.0 %all-to-all-start = ((bf16[256,32,128]{2,1,0:T(8,128)(2,1)}), bf16[256,32,128]{2,1,0:T(8,128)(2,1)S(1)}, u32[]{:S(2)}, u32[]{:S(2)}) async-start(bf16[256,32,128]{2,1,0:T(8,128)(2,1)} %bitcast.4), calls=%async_computation | async-start | bytes 4194304 | tf_op jit(solution)/shard_map/all_to_all | solution.py:463
  81.6 14.3 %all-to-all-start.1 = ((f32[8,136,128]{2,1,0:T(8,128)}), f32[8,136,128]{2,1,0:T(8,128)S(1)}, u32[]{:S(2)}, u32[]{:S(2)}) async-start(f32[8,136,128]{2,1,0:T(8,128)} %get-tuple-element.20.own_ref), calls=%async_computation.1 | async-start | bytes 1114112 | tf_op jit(solution)/shard_map/all_to_all | solution.py:468
  85.3 18.4 %copy-start.2 = (s32[2]{0:T(128)S(1)}, s32[2]{0:T(128)}, u32[]{:S(2)}) copy-start(s32[2]{0:T(128)} %param.7) | copy-start | bytes 28
  85.3 31.5 %copy-start = (s32[32,128]{1,0:T(8,128)S(1)}, s32[32,128]{1,0:T(8,128)}, u32[]{:S(2)}) copy-start(s32[32,128]{1,0:T(8,128)} %get-tuple-element.22.target_ref) | copy-start | bytes 49156
  95.9 20.8 %all-to-all-start.2 = ((f32[256,1,128]{2,1,0:T(1,128)}), f32[256,1,128]{2,1,0:T(1,128)S(1)}, u32[]{:S(2)}, u32[]{:S(2)}) async-start(f32[256,1,128]{2,1,0:T(1,128)} %bitcast.2), calls=%async_computation.2 | async-start | bytes 262144 | tf_op jit(solution)/shard_map/all_to_all | solution.py:471
